TPU v7x, 32 devices: a whole 2x2x4 slice. The times are simulated.
32 devices in a mesh: rows: 8 (over z, y), cols: 4 (over x, core).
Axes of the slice: x: 2, y: 2, z: 4, core: 2. Of those that a mesh axis runs over, the one named last changes fastest.
Arguments:
- trace_limbs: float32 [2, 33554432], P(None, ('cols', 'rows')), parts along dimension 1, may hold values from 0 to 1, as said below
- coset_shift: int32 [1], replicated, may hold values from 1 to 2013265920
Outputs:
- extension: float32 [2, 67108864], P(None, ('cols', 'rows')), parts along dimension 1
There are 4 independent parts, one for each index of `cols`. A program takes and returns all parts, laid end to end along the dimension named above; an argument that names none is the same for every part. Nothing has to cross between parts.
Inputs may be any that keep to these rules, and one draw needn't show every extreme that they name: `trace_limbs`: every entry is a whole multiple of 2**-16, and the entries of the second limb row are below one half.
All inputs are finite; a program needn't handle non-finite values.
Results may differ from a plain program's by a relative error of at most 0.0003.
Values may be sent and summed in bfloat16 or wider, within the bound.
A program may use at most 192 MiB of HBM per device.

v0:
```python
import jax
import jax.numpy as jnp
from jax import lax
from jax.sharding import PartitionSpec as P

LEN_A = 2048
LEN_B = 4096


MODULUS = 2013265921


def unity_root(length):
    return pow(pow(31, 15, MODULUS), (1 << 27) // length, MODULUS)


def reduce_product(small_factor, field_factor):
    estimate = jnp.floor(
        small_factor.astype(jnp.float32) * field_factor.astype(jnp.float32) * (1.0 / MODULUS) + 0.5
    )
    remainder = small_factor * field_factor - estimate.astype(jnp.int32) * MODULUS
    return jnp.where(remainder < 0, remainder + MODULUS, remainder)


def field_add(first_term, second_term):
    summed = first_term - MODULUS + second_term
    return jnp.where(summed < 0, summed + MODULUS, summed)


def field_sub(first_term, second_term):
    differ = first_term - second_term
    return jnp.where(differ < 0, differ + MODULUS, differ)


def field_mul(factor_one, factor_two):
    high_part = reduce_product(factor_one >> 16, factor_two)
    low_part = reduce_product(factor_one & 65535, factor_two)
    return field_add(reduce_product(jnp.int32(65536), high_part), low_part)


def paired_mul(factor_one, table_plain, table_lifted):
    high_part = reduce_product(factor_one >> 16, table_lifted)
    low_part = reduce_product(factor_one & 65535, table_plain)
    return field_add(high_part, low_part)


def const_powers(base_value, exponents, bit_count):
    result = jnp.ones_like(exponents)
    for bit_level in range(bit_count):
        factor = jnp.where(
            exponents >> bit_level & 1 == 1,
            jnp.int32(pow(base_value, 1 << bit_level, MODULUS)),
            jnp.int32(1),
        )
        result = field_mul(result, factor)
    return result


def traced_powers(base_value, exponents, bit_count):
    result = jnp.ones_like(exponents)
    square = base_value
    for bit_level in range(bit_count):
        result = jnp.where(exponents >> bit_level & 1 == 1, field_mul(result, square), result)
        square = field_mul(square, square)
    return result


def power_table(base_value, length):
    low_count = min(64, length)
    low_part = const_powers(base_value, jnp.arange(low_count, dtype=jnp.int32), 6)
    high_count = length // low_count
    high_part = const_powers(
        pow(base_value, low_count, MODULUS),
        jnp.arange(high_count, dtype=jnp.int32),
        max(1, high_count.bit_length()),
    )
    plain = field_mul(high_part[:, None], low_part[None, :]).reshape(length)
    return (plain, field_mul(plain, jnp.int32(65536)))


def transform(values, root_pair):
    table_plain, table_lifted = root_pair
    length = values.shape[-1]
    row_count = values.size // length
    state = values.reshape(row_count, length)
    leading = state.T.reshape(1, length * row_count)
    half_span = 1
    while half_span < length and half_span < 128:
        groups = length // (2 * half_span)
        halves = leading.reshape(half_span, 2, groups * row_count)
        even_part = halves[:, 0]
        odd_part = halves[:, 1]
        product = paired_mul(
            odd_part, table_plain[::groups][:, None], table_lifted[::groups][:, None]
        )
        leading = jnp.stack(
            [field_add(even_part, product), field_sub(even_part, product)], 0
        ).reshape(2 * half_span, groups * row_count)
        half_span = half_span * 2
    state = (
        leading.reshape(half_span, length // half_span, row_count)
        .transpose(2, 1, 0)
        .reshape(row_count, length)
    )
    while half_span < length:
        groups = length // (2 * half_span)
        halves = state.reshape(row_count, 2, length // 2)
        even_part = halves[:, 0]
        odd_part = halves[:, 1]
        plain_row = jnp.tile(table_plain[::groups], groups)
        lifted_row = jnp.tile(table_lifted[::groups], groups)
        product = paired_mul(odd_part, plain_row[None, :], lifted_row[None, :])
        sum_part = field_add(even_part, product).reshape(row_count, groups, half_span)
        diff_part = field_sub(even_part, product).reshape(row_count, groups, half_span)
        state = jnp.stack([sum_part, diff_part], 2).reshape(row_count, length)
        half_span = half_span * 2
    return state.reshape(values.shape)


def cross_twiddle(root_value, line_ids, width, modulus_len):
    bit_count = (modulus_len - 1).bit_length()
    fine_exp = jnp.arange(64, dtype=jnp.int32)
    coarse = jnp.arange(width // 64, dtype=jnp.int32) * 64
    fine_part = const_powers(
        root_value, line_ids[:, None] * fine_exp[None, :] & modulus_len - 1, bit_count
    )
    coarse_part = const_powers(
        root_value, line_ids[:, None] * coarse[None, :] & modulus_len - 1, bit_count
    )
    return field_mul(coarse_part[:, :, None], fine_part[:, None, :]).reshape(
        line_ids.shape[0], width
    )


def from_limbs(trace_limbs):
    low_part = (trace_limbs[0] * 65536.0).astype(jnp.int32)
    high_part = (trace_limbs[1] * 65536.0).astype(jnp.int32)
    joined = high_part * 65536 + low_part
    return jnp.where(joined >= MODULUS, joined - MODULUS, joined)


def to_limbs(field_values):
    return (
        jnp.stack(
            [(field_values & 65535).astype(jnp.float32), (field_values >> 16).astype(jnp.float32)]
        )
        / 65536.0
    )


def regroup_map(matrix, devices, worker):
    line_count = matrix.shape[1] // devices
    blocks = matrix.T.reshape(devices, line_count, matrix.shape[0])
    moved = worker(lax.all_to_all(blocks, "rows", split_axis=0, concat_axis=2, tiled=True))
    return moved.reshape(line_count, moved.shape[2])


def regroup(matrix, devices):
    line_count = matrix.shape[1] // devices
    blocks = matrix.T.reshape(devices, line_count, matrix.shape[0])
    moved = lax.all_to_all(blocks, "rows", split_axis=0, concat_axis=2, tiled=True)
    return moved.reshape(line_count * moved.shape[2])


def on_device(trace_limbs, coset_shift):
    devices = lax.axis_size("rows")
    position = lax.axis_index("rows")
    values = from_limbs(trace_limbs)
    first_len = LEN_A
    second_len = LEN_B
    longer = 2 * LEN_B
    trace_len = first_len * second_len
    ext_len = 2 * trace_len
    rows_a = first_len // devices
    rows_b = second_len // devices
    rows_long = longer // devices
    back_root = pow(unity_root(trace_len), MODULUS - 2, MODULUS)
    first_back = power_table(pow(unity_root(first_len), MODULUS - 2, MODULUS), first_len // 2)
    second_back = power_table(pow(unity_root(second_len), MODULUS - 2, MODULUS), second_len // 2)
    first_fwd = power_table(unity_root(first_len), first_len // 2)
    long_fwd = power_table(unity_root(longer), longer // 2)

    def first_back_pass(block_in):
        return transform(block_in, first_back)

    def second_back_pass(block_in):
        return transform(block_in, second_back)

    def padded_pass(block_in):
        return transform(jnp.concatenate([block_in, jnp.zeros_like(block_in)], -1), first_fwd)

    def long_pass(block_in):
        return transform(block_in, long_fwd)

    matrix = values.reshape(rows_a, second_len)
    columns = regroup_map(matrix, devices, first_back_pass)
    col_ids = position * rows_b + jnp.arange(rows_b, dtype=jnp.int32)
    columns = field_mul(columns, cross_twiddle(back_root, col_ids, first_len, trace_len))
    rows_back = regroup_map(columns, devices, second_back_pass)
    inverse_len = jnp.int32(pow(trace_len, MODULUS - 2, MODULUS))
    shift_base = coset_shift[0]
    shift_first = traced_powers(
        shift_base, jnp.array([first_len], dtype=jnp.int32), first_len.bit_length()
    )[0]
    ordered = regroup(rows_back, devices).reshape(rows_b, first_len)
    inner_powers = field_mul(
        traced_powers(shift_base, jnp.arange(first_len, dtype=jnp.int32), first_len.bit_length()),
        inverse_len,
    )
    outer_powers = traced_powers(shift_first, col_ids, second_len.bit_length())
    shifted = field_mul(ordered, field_mul(outer_powers[:, None], inner_powers[None, :]))
    rows_half = first_len // (2 * devices)
    spread = regroup_map(shifted.reshape(rows_half, longer), devices, padded_pass)
    long_ids = position * rows_long + jnp.arange(rows_long, dtype=jnp.int32)
    spread = field_mul(spread, cross_twiddle(unity_root(ext_len), long_ids, first_len, ext_len))
    gathered = regroup_map(spread, devices, long_pass)
    extended = regroup(gathered, devices)
    return to_limbs(extended)


def solution(mesh):
    placed = (P(None, ("cols", "rows")), P())
    return jax.shard_map(
        on_device, mesh=mesh, in_specs=placed, out_specs=P(None, ("cols", "rows")), check_vma=False
    )
```

profile of v0, /device:TPU:0, one launch (start us, length us, event | category | flops | bytes accessed | tf_op | source)
XLA Modules:
  0.0 2819.0 jit_solution(12654533971246297878)
XLA Ops:
  0.0 39.0 %add_reduce_fusion = s32[1048576]{0:T(1024)} fusion(f32[2,1048576]{1,0:T(2,128)} %param.3), kind=kLoop, calls=%fused_computation.693 | loop fusion | flops 6291456 | bytes 12582912 | tf_op jit(solution)/shard_map/add | solution.py:138
  102.9 52.6 %all-to-all-done = s32[8,512,256]{2,1,0:T(8,128)} async-done(((s32[8,512,256]{2,1,0:T(8,128)}), s32[8,512,256]{2,1,0:T(8,128)}, u32[]{:S(2)}, u32[]{:S(2)}) %all-to-all-start) | async-done | bytes 4194336 | tf_op jit(solution)/shard_map/all_to_all | solution.py:154
  168.7 24.8 compare_select_fusion.134
  223.4 23.8 compare_select_fusion.129
  308.0 23.5 compare_select_fusion.119
  350.0 23.6 compare_select_fusion.114
  392.3 23.6 compare_select_fusion.109
  476.4 86.2 %all-to-all-done.1 = s32[8,256,512]{2,1,0:T(8,128)} async-done(((s32[8,256,512]{2,1,0:T(8,128)}), s32[8,256,512]{2,1,0:T(8,128)}, u32[]{:S(2)}, u32[]{:S(2)}) %all-to-all-start.1) | async-done | bytes 4194336 | tf_op jit(solution)/shard_map/all_to_all | solution.py:154
  574.9 25.0 compare_select_fusion.104
  629.7 23.8 compare_select_fusion.99
  756.1 23.6 compare_select_fusion.84
  798.6 23.6 compare_select_fusion.79
  889.9 65.4 %all-to-all-done.2 = s32[8,512,256]{2,1,0:T(8,128)} async-done(((s32[8,512,256]{2,1,0:T(8,128)}), s32[8,512,256]{2,1,0:T(8,128)}, u32[]{:S(2)}, u32[]{:S(2)}) %all-to-all-start.2) | async-done | bytes 4194336 | tf_op jit(solution)/shard_map/all_to_all | solution.py:161
  1036.9 40.3 %fusion.2297 = (f32[1024,64]{0,1:T(8,128)S(1)}, s32[1024,64]{0,1:T(8,128)S(1)}) fusion(s32[1024]{0:T(1024)S(1)} %iota_add_fusion), kind=kLoop, calls=%fused_computation.3961 | loop fusion | flops 73662464 | bytes 528384 | tf_op jit(solution)/shard_map/convert_element_type | solution.py:19
  1117.4 47.1 %compare_select_fusion.56 = (s32[1,1,1048576]{2,1,0:T(1,128)S(1)}, s32[1,1,1048576]{2,1,0:T(1,128)S(1)}) fusion(s32[1,2,1048576]{2,1,0:T(2,128)} %reshape_reshape.169, f32[]{:T(128)} %bitcast.153, s32[]{:T(128)} %bitcast.152, f32[]{:T(128)} %bitcast.151, s32[]{:T(128)} %bitcast.150), kind=kLoop, calls=%fused_computation.56 | loop fusion | flops 37748736 | bytes 16777232 | tf_op jit(solution)/shard_map/jit(_where)/select_n | solution.py:27
  1171.4 26.0 compare_select_fusion.74
  1220.6 46.5 %compare_select_fusion.51 = (s32[1,4,262144]{2,0,1:T(1,128)S(1)}, s32[1,4,262144]{2,0,1:T(1,128)S(1)}) fusion(s32[4,2,262144]{2,1,0:T(2,128)} %reshape_reshape.170, f32[4]{0:T(128)S(1)} %convert_element_type.43101, s32[4]{0:T(128)S(1)} %slice.811, f32[4]{0:T(128)S(1)} %convert_element_type.43098, s32[4]{0:T(128)S(1)} %slice.810), kind=kLoop, calls=%fused_computation.51 | loop fusion | flops 37748736 | bytes 16777280 | tf_op jit(solution)/shard_map/jit(_where)/select_n | solution.py:27
  1303.8 46.1 %compare_select_fusion.46 = (s32[1,8,131072]{2,0,1:T(1,128)S(1)}, s32[1,8,131072]{2,0,1:T(1,128)S(1)}) fusion(s32[8,2,131072]{2,1,0:T(2,128)} %reshape_reshape.171, f32[8]{0:T(128)S(1)} %convert_element_type.43107, s32[8]{0:T(128)S(1)} %slice.815, f32[8]{0:T(128)S(1)} %convert_element_type.43104, s32[8]{0:T(128)S(1)} %slice.814), kind=kLoop, calls=%fused_computation.46 | loop fusion | flops 37748736 | bytes 16777344 | tf_op jit(solution)/shard_map/jit(_where)/select_n | solution.py:27
  1384.1 46.3 %compare_select_fusion.41 = (s32[1,16,65536]{2,0,1:T(1,128)S(1)}, s32[1,16,65536]{2,0,1:T(1,128)S(1)}) fusion(s32[16,2,65536]{2,1,0:T(2,128)} %reshape_reshape.172, f32[16]{0:T(128)S(1)} %convert_element_type.43113, s32[16]{0:T(128)S(1)} %slice.819, f32[16]{0:T(128)S(1)} %convert_element_type.43110, s32[16]{0:T(128)S(1)} %slice.818), kind=kLoop, calls=%fused_computation.41 | loop fusion | flops 37748736 | bytes 16777472 | tf_op jit(solution)/shard_map/jit(_where)/select_n | solution.py:27
  1463.9 46.5 %compare_select_fusion.36 = (s32[1,32,32768]{2,0,1:T(1,128)S(1)}, s32[1,32,32768]{2,0,1:T(1,128)S(1)}) fusion(s32[32,2,32768]{2,1,0:T(2,128)} %reshape_reshape.173, f32[32]{0:T(128)S(1)} %convert_element_type.43119, s32[32]{0:T(128)S(1)} %slice.823, f32[32]{0:T(128)S(1)} %convert_element_type.43116, s32[32]{0:T(128)S(1)} %slice.822), kind=kLoop, calls=%fused_computation.36 | loop fusion | flops 37748736 | bytes 16777728 | tf_op jit(solution)/shard_map/jit(_where)/select_n | solution.py:27
  1544.4 46.2 %compare_select_fusion.31 = (s32[1,64,16384]{2,0,1:T(1,128)S(1)}, s32[1,64,16384]{2,0,1:T(1,128)S(1)}) fusion(s32[64,2,16384]{2,1,0:T(2,128)} %reshape_reshape.174, f32[64]{0:T(128)S(1)} %convert_element_type.43125, s32[64]{0:T(128)S(1)} %slice.827, f32[64]{0:T(128)S(1)} %convert_element_type.43122, s32[64]{0:T(128)S(1)} %slice.826), kind=kLoop, calls=%fused_computation.31 | loop fusion | flops 37748736 | bytes 16778240 | tf_op jit(solution)/shard_map/jit(_where)/select_n | solution.py:27
  1728.6 168.1 %all-to-all-done.4 = s32[8,256,1024]{2,1,0:T(8,128)} async-done(((s32[8,256,1024]{2,1,0:T(8,128)}), s32[8,256,1024]{2,1,0:T(8,128)}, u32[]{:S(2)}, u32[]{:S(2)}) %all-to-all-start.4) | async-done | bytes 8388640 | tf_op jit(solution)/shard_map/all_to_all | solution.py:154
  1918.3 47.1 %compare_select_fusion.26 = (s32[1,1,1048576]{2,1,0:T(1,128)S(1)}, s32[1,1,1048576]{2,1,0:T(1,128)S(1)}) fusion(s32[1,2,1048576]{2,1,0:T(2,128)} %reshape_reshape.180, f32[]{:T(128)} %bitcast.216, s32[]{:T(128)} %bitcast.215, f32[]{:T(128)} %bitcast.214, s32[]{:T(128)} %bitcast.213), kind=kLoop, calls=%fused_computation.26 | loop fusion | flops 37748736 | bytes 16777232 | tf_op jit(solution)/shard_map/jit(_where)/select_n | solution.py:27
  1972.2 26.2 compare_select_fusion.69
  2021.7 46.4 %compare_select_fusion.21 = (s32[1,4,262144]{2,0,1:T(1,128)S(1)}, s32[1,4,262144]{2,0,1:T(1,128)S(1)}) fusion(s32[4,2,262144]{2,1,0:T(2,128)} %reshape_reshape.181, f32[4]{0:T(128)S(1)} %convert_element_type.43613, s32[4]{0:T(128)S(1)} %slice.853, f32[4]{0:T(128)S(1)} %convert_element_type.43610, s32[4]{0:T(128)S(1)} %slice.852), kind=kLoop, calls=%fused_computation.21 | loop fusion | flops 37748736 | bytes 16777280 | tf_op jit(solution)/shard_map/jit(_where)/select_n | solution.py:27
  2104.7 45.9 %compare_select_fusion.16 = (s32[1,8,131072]{2,0,1:T(1,128)S(1)}, s32[1,8,131072]{2,0,1:T(1,128)S(1)}) fusion(s32[8,2,131072]{2,1,0:T(2,128)} %reshape_reshape.182, f32[8]{0:T(128)S(1)} %convert_element_type.43619, s32[8]{0:T(128)S(1)} %slice.857, f32[8]{0:T(128)S(1)} %convert_element_type.43616, s32[8]{0:T(128)S(1)} %slice.856), kind=kLoop, calls=%fused_computation.16 | loop fusion | flops 37748736 | bytes 16777344 | tf_op jit(solution)/shard_map/jit(_where)/select_n | solution.py:27
  2184.5 46.4 %compare_select_fusion.11 = (s32[1,16,65536]{2,0,1:T(1,128)S(1)}, s32[1,16,65536]{2,0,1:T(1,128)S(1)}) fusion(s32[16,2,65536]{2,1,0:T(2,128)} %reshape_reshape.183, f32[16]{0:T(128)S(1)} %convert_element_type.43625, s32[16]{0:T(128)S(1)} %slice.861, f32[16]{0:T(128)S(1)} %convert_element_type.43622, s32[16]{0:T(128)S(1)} %slice.860), kind=kLoop, calls=%fused_computation.11 | loop fusion | flops 37748736 | bytes 16777472 | tf_op jit(solution)/shard_map/jit(_where)/select_n | solution.py:27
  2264.5 46.0 %compare_select_fusion.6 = (s32[1,32,32768]{2,0,1:T(1,128)S(1)}, s32[1,32,32768]{2,0,1:T(1,128)S(1)}) fusion(s32[32,2,32768]{2,1,0:T(2,128)} %reshape_reshape.184, f32[32]{0:T(128)S(1)} %convert_element_type.43631, s32[32]{0:T(128)S(1)} %slice.865, f32[32]{0:T(128)S(1)} %convert_element_type.43628, s32[32]{0:T(128)S(1)} %slice.864), kind=kLoop, calls=%fused_computation.6 | loop fusion | flops 37748736 | bytes 16777728 | tf_op jit(solution)/shard_map/jit(_where)/select_n | solution.py:27
  2344.5 45.9 %compare_select_fusion.1 = (s32[1,64,16384]{2,0,1:T(1,128)S(1)}, s32[1,64,16384]{2,0,1:T(1,128)S(1)}) fusion(s32[64,2,16384]{2,1,0:T(2,128)} %reshape_reshape.185, f32[64]{0:T(128)S(1)} %convert_element_type.43637, s32[64]{0:T(128)S(1)} %slice.869, f32[64]{0:T(128)S(1)} %convert_element_type.43634, s32[64]{0:T(128)S(1)} %slice.868), kind=kLoop, calls=%fused_computation.1 | loop fusion | flops 37748736 | bytes 16778240 | tf_op jit(solution)/shard_map/jit(_where)/select_n | solution.py:27
  2512.2 186.8 %all_to_all.81 = s32[8,1024,256]{2,1,0:T(8,128)} all-to-all(s32[8,1024,256]{2,1,0:T(8,128)S(1)} %bitcast.1943), channel_id=1, replica_groups=mesh['rows'=8,'cols'=4] {'rows'}, dimensions={0} | all-to-all | bytes 16777216 | tf_op jit(solution)/shard_map/all_to_all | solution.py:161
  2718.5 37.9 %copy.409 = f32[1,1,8192,256]{3,1,2,0:T(1,128)} copy(f32[1,1,8192,256]{3,2,1,0:T(8,128)S(1)} %bitcast.1949) | data formatting | bytes 16777216
  2761.2 37.7 %copy.410 = f32[1,1,8192,256]{3,1,2,0:T(1,128)} copy(f32[1,1,8192,256]{3,2,1,0:T(8,128)S(1)} %bitcast.1950) | data formatting | bytes 16777216
  (617 shorter events, 1271.0 us)
Async XLA Ops:
  54.7 100.8 %all-to-all-start = ((s32[8,512,256]{2,1,0:T(8,128)}), s32[8,512,256]{2,1,0:T(8,128)}, u32[]{:S(2)}, u32[]{:S(2)}) async-start(s32[8,512,256]{2,1,0:T(8,128)} %bitcast.1988), calls=%async_computation | async-start | bytes 8388608 | tf_op jit(solution)/shard_map/all_to_all | solution.py:154
  465.4 97.1 %all-to-all-start.1 = ((s32[8,256,512]{2,1,0:T(8,128)}), s32[8,256,512]{2,1,0:T(8,128)}, u32[]{:S(2)}, u32[]{:S(2)}) async-start(s32[8,256,512]{2,1,0:T(8,128)} %bitcast.1981), calls=%async_computation.1 | async-start | bytes 8388608 | tf_op jit(solution)/shard_map/all_to_all | solution.py:154
  858.2 97.1 %all-to-all-start.2 = ((s32[8,512,256]{2,1,0:T(8,128)}), s32[8,512,256]{2,1,0:T(8,128)}, u32[]{:S(2)}, u32[]{:S(2)}) async-start(s32[8,512,256]{2,1,0:T(8,128)} %bitcast.1987), calls=%async_computation.2 | async-start | bytes 8388608 | tf_op jit(solution)/shard_map/all_to_all | solution.py:161
  999.5 97.2 %all-to-all-start.3 = ((s32[8,1024,128]{1,2,0:T(8,128)}), s32[8,1024,128]{1,2,0:T(8,128)}, u32[]{:S(2)}, u32[]{:S(2)}) async-start(s32[8,1024,128]{1,2,0:T(8,128)} %bitcast.1989), calls=%async_computation.3 | async-start | bytes 8388608 | tf_op jit(solution)/shard_map/all_to_all | solution.py:154
  1005.4 80.4 %copy-start.36 = (s32[1024]{0:T(1024)}, s32[1024]{0:T(1024)S(1)}, u32[]{:S(2)}) copy-start(s32[1024]{0:T(1024)S(1)} %get-tuple-element.42) | copy-start | bytes 12292
  1005.4 80.4 %copy-start.44 = (s32[1024]{0:T(1024)}, s32[1024]{0:T(1024)S(1)}, u32[]{:S(2)}) copy-start(s32[1024]{0:T(1024)S(1)} %get-tuple-element.41) | copy-start | bytes 12292
  1008.0 77.8 %copy-start.76 = (s32[128]{0:T(128)}, s32[128]{0:T(128)S(1)}, u32[]{:S(2)}) copy-start(s32[128]{0:T(128)S(1)} %slice.831) | copy-start | bytes 1540
  1008.3 77.6 %copy-start.78 = (s32[128]{0:T(128)}, s32[128]{0:T(128)S(1)}, u32[]{:S(2)}) copy-start(s32[128]{0:T(128)S(1)} %slice.830) | copy-start | bytes 1540
  1008.5 77.3 %copy-start.58 = (s32[256]{0:T(256)}, s32[256]{0:T(256)S(1)}, u32[]{:S(2)}) copy-start(s32[256]{0:T(256)S(1)} %slice.835) | copy-start | bytes 3076
  1008.7 77.1 %copy-start.60 = (s32[256]{0:T(256)}, s32[256]{0:T(256)S(1)}, u32[]{:S(2)}) copy-start(s32[256]{0:T(256)S(1)} %slice.834) | copy-start | bytes 3076
  1008.9 76.9 %copy-start.46 = (s32[512]{0:T(512)}, s32[512]{0:T(512)S(1)}, u32[]{:S(2)}) copy-start(s32[512]{0:T(512)S(1)} %slice.839) | copy-start | bytes 6148
  1009.1 76.7 %copy-start.48 = (s32[512]{0:T(512)}, s32[512]{0:T(512)S(1)}, u32[]{:S(2)}) copy-start(s32[512]{0:T(512)S(1)} %slice.838) | copy-start | bytes 6148
  1117.4 47.1 %copy-start = (s32[1,2,1048576]{2,1,0:T(2,128)S(1)}, s32[1,2,1048576]{2,1,0:T(2,128)}, u32[]{:S(2)}) copy-start(s32[1,2,1048576]{2,1,0:T(2,128)} %reshape_reshape.169) | copy-start | bytes 25165828
  1220.6 46.6 %copy-start.1 = (s32[4,2,262144]{2,1,0:T(2,128)S(1)}, s32[4,2,262144]{2,1,0:T(2,128)}, u32[]{:S(2)}) copy-start(s32[4,2,262144]{2,1,0:T(2,128)} %reshape_reshape.170) | copy-start | bytes 25165828
  1384.1 46.3 %copy-start.3 = (s32[16,2,65536]{2,1,0:T(2,128)S(1)}, s32[16,2,65536]{2,1,0:T(2,128)}, u32[]{:S(2)}) copy-start(s32[16,2,65536]{2,1,0:T(2,128)} %reshape_reshape.172) | copy-start | bytes 25165828
  1463.9 46.5 %copy-start.4 = (s32[32,2,32768]{2,1,0:T(2,128)S(1)}, s32[32,2,32768]{2,1,0:T(2,128)}, u32[]{:S(2)}) copy-start(s32[32,2,32768]{2,1,0:T(2,128)} %reshape_reshape.173) | copy-start | bytes 25165828
  1709.5 187.2 %all-to-all-start.4 = ((s32[8,256,1024]{2,1,0:T(8,128)}), s32[8,256,1024]{2,1,0:T(8,128)}, u32[]{:S(2)}, u32[]{:S(2)}) async-start(s32[8,256,1024]{2,1,0:T(8,128)} %bitcast.1930), calls=%async_computation.4 | async-start | bytes 16777216 | tf_op jit(solution)/shard_map/all_to_all | solution.py:154
  1715.8 190.0 %copy-start.26 = (s32[4096]{0:T(1024)}, s32[4096]{0:T(1024)S(1)}, u32[]{:S(2)}) copy-start(s32[4096]{0:T(1024)S(1)} %get-tuple-element.7) | copy-start | bytes 49156
  1715.8 190.0 %copy-start.28 = (s32[4096]{0:T(1024)}, s32[4096]{0:T(1024)S(1)}, u32[]{:S(2)}) copy-start(s32[4096]{0:T(1024)S(1)} %get-tuple-element.6) | copy-start | bytes 49156
  1718.5 187.3 %copy-start.82 = (s32[128]{0:T(128)}, s32[128]{0:T(128)S(1)}, u32[]{:S(2)}) copy-start(s32[128]{0:T(128)S(1)} %slice.873) | copy-start | bytes 1540
  1718.7 187.1 %copy-start.84 = (s32[128]{0:T(128)}, s32[128]{0:T(128)S(1)}, u32[]{:S(2)}) copy-start(s32[128]{0:T(128)S(1)} %slice.872) | copy-start | bytes 1540
  1718.9 186.9 %copy-start.62 = (s32[256]{0:T(256)}, s32[256]{0:T(256)S(1)}, u32[]{:S(2)}) copy-start(s32[256]{0:T(256)S(1)} %slice.877) | copy-start | bytes 3076
  1719.1 186.7 %copy-start.64 = (s32[256]{0:T(256)}, s32[256]{0:T(256)S(1)}, u32[]{:S(2)}) copy-start(s32[256]{0:T(256)S(1)} %slice.876) | copy-start | bytes 3076
  1719.4 186.5 %copy-start.50 = (s32[512]{0:T(512)}, s32[512]{0:T(512)S(1)}, u32[]{:S(2)}) copy-start(s32[512]{0:T(512)S(1)} %slice.881) | copy-start | bytes 6148
  1719.6 186.3 %copy-start.52 = (s32[512]{0:T(512)}, s32[512]{0:T(512)S(1)}, u32[]{:S(2)}) copy-start(s32[512]{0:T(512)S(1)} %slice.880) | copy-start | bytes 6148
  1719.8 186.1 %copy-start.38 = (s32[1024]{0:T(1024)}, s32[1024]{0:T(1024)S(1)}, u32[]{:S(2)}) copy-start(s32[1024]{0:T(1024)S(1)} %slice.885) | copy-start | bytes 12292
  1720.0 185.9 %copy-start.40 = (s32[1024]{0:T(1024)}, s32[1024]{0:T(1024)S(1)}, u32[]{:S(2)}) copy-start(s32[1024]{0:T(1024)S(1)} %slice.884) | copy-start | bytes 12292
  1720.4 185.5 %copy-start.30 = (s32[2048]{0:T(1024)}, s32[2048]{0:T(1024)S(1)}, u32[]{:S(2)}) copy-start(s32[2048]{0:T(1024)S(1)} %slice.889) | copy-start | bytes 24580
  1720.7 185.2 %copy-start.32 = (s32[2048]{0:T(1024)}, s32[2048]{0:T(1024)S(1)}, u32[]{:S(2)}) copy-start(s32[2048]{0:T(1024)S(1)} %slice.888) | copy-start | bytes 24580
  1918.3 47.1 %copy-start.6 = (s32[1,2,1048576]{2,1,0:T(2,128)S(1)}, s32[1,2,1048576]{2,1,0:T(2,128)}, u32[]{:S(2)}) copy-start(s32[1,2,1048576]{2,1,0:T(2,128)} %reshape_reshape.180) | copy-start | bytes 25165828
  2021.7 46.4 %copy-start.7 = (s32[4,2,262144]{2,1,0:T(2,128)S(1)}, s32[4,2,262144]{2,1,0:T(2,128)}, u32[]{:S(2)}) copy-start(s32[4,2,262144]{2,1,0:T(2,128)} %reshape_reshape.181) | copy-start | bytes 25165828
  2184.5 46.4 %copy-start.9 = (s32[16,2,65536]{2,1,0:T(2,128)S(1)}, s32[16,2,65536]{2,1,0:T(2,128)}, u32[]{:S(2)}) copy-start(s32[16,2,65536]{2,1,0:T(2,128)} %reshape_reshape.183) | copy-start | bytes 25165828
  (65 other events, 821.8 us)
where the time goes:
time: 2830 us; the launch traced here: 2820 us
  other arithmetic  1630 us (58%)
  local copies, waits for them, and re-layouts  579 us (20%)
  waiting for transfers between devices  383 us (14%)
  blocking collectives  187 us (7%)
    select_n x50, other arithmetic, field_add(): return jnp.where(summed < 0, summed + MODULUS, summed)  1090 us
    all_to_all x4, waiting for transfers between devices, regroup_map(): lax.all_to_all(blocks, 'rows', split_axis=0, concat_axis=2, tiled=True)  318 us
    another operation x24, local copies, waits for them, and re-layouts, transform(): halves = leading.reshape(half_span, 2, groups * row_count)  234 us
    all_to_all x1, blocking collectives, regroup(): lax.all_to_all(blocks, 'rows', split_axis=0, concat_axis=2, tiled=True)  187 us
    select_n x43, other arithmetic, field_sub(): return jnp.where(differ < 0, differ + MODULUS, differ)  159 us
    another operation x20, local copies, waits for them, and re-layouts, transform(): jnp.stack([field_add(even_part, product), field_sub(even_part, product)], 0)  120 us
    another operation x24, other arithmetic, transform(): jnp.stack([field_add(even_part, product), field_sub(even_part, product)], 0)  117 us
    unnamed x198, local copies, waits for them, and re-layouts  114 us
  transfers between devices with their start and end apart: 5, of which 5 were waited for; matrix products, arithmetic and copies ran while one was open for 6% of the time, Pallas kernels for 0%

commit v1 on v0

v1 whole, which is shorter than its diff:
```python
import functools

import jax
import jax.numpy as jnp
import numpy as np
from jax import lax
from jax.experimental import pallas as pl
from jax.experimental.pallas import tpu as pltpu
from jax.sharding import PartitionSpec as P

MODULUS = 2013265921
LOG_TRACE = 23
TRACE_LEN = 1 << LOG_TRACE
VMEM_BYTES = 56 * 1024 * 1024


def unity_root(length):
    return pow(pow(31, 15, MODULUS), (1 << 27) // length, MODULUS)


def inverse_of(value):
    return pow(value, MODULUS - 2, MODULUS)


def np_powers(base, count):
    table = np.ones(1, np.uint64)
    step = base
    while table.size < count:
        table = np.concatenate([table, table * np.uint64(step) % np.uint64(MODULUS)])
        step = step * step % MODULUS
    return table[:count].astype(np.int64)


def centred(values):
    return np.where(values > MODULUS // 2, values - MODULUS, values)


def np_pair(values):
    values = np.asarray(values, np.int64) % MODULUS
    lifted = values * 65536 % MODULUS
    return centred(values).astype(np.int32), centred(lifted).astype(np.int32)


def np_digits(values):
    digits = []
    rest = centred(np.asarray(values, np.int64) % MODULUS)
    for _ in range(3):
        above = (rest + 128) >> 8
        digits.append(rest - (above << 8))
        rest = above
    return digits + [rest]


def np_left_matrix(base):
    lifted = [base * (1 << (8 * a)) % MODULUS for a in range(4)]
    wide = np.concatenate(lifted, 1)
    return np.concatenate(np_digits(wide), 0).astype(jnp.bfloat16)


def np_right_matrix(base):
    lifted = [base * (1 << (8 * a)) % MODULUS for a in range(4)]
    tall = np.concatenate(lifted, 0)
    return np.concatenate(np_digits(tall), 1).astype(jnp.bfloat16)


def outer_powers(root, rows, columns, order):
    table = np_powers(root, order)
    exponents = np.arange(rows)[:, None] * np.arange(columns)[None, :]
    return table[exponents % order]


def times(x, plain, lifted):
    high = x >> 16
    low = x & 65535
    scale = jnp.float32(1.0 / MODULUS)
    estimate = high.astype(jnp.float32) * (lifted.astype(jnp.float32) * scale) + low.astype(
        jnp.float32
    ) * (plain.astype(jnp.float32) * scale)
    quotient = jnp.floor(estimate + 0.5).astype(jnp.int32)
    return high * lifted + low * plain - quotient * jnp.int32(MODULUS)


def times_const(x, value):
    plain, lifted = np_pair(np.int64(value))
    return times(x, jnp.int32(int(plain)), jnp.int32(int(lifted)))


def lift(x):
    return times_const(x, 65536)


def split_digits(x):
    digits = []
    for _ in range(3):
        above = (x + 128) >> 8
        digits.append((x - (above << 8)).astype(jnp.float32).astype(jnp.bfloat16))
        x = above
    return digits + [x.astype(jnp.float32).astype(jnp.bfloat16)]


def join_sums(sums):
    scale = 1.0 / MODULUS
    estimate = sums[0] * jnp.float32(scale)
    total = sums[0].astype(jnp.int32)
    for place in range(1, 4):
        estimate = estimate + sums[place] * jnp.float32(scale * (1 << (8 * place)))
        total = total + (sums[place].astype(jnp.int32) << (8 * place))
    quotient = jnp.floor(estimate + 0.5).astype(jnp.int32)
    return total - quotient * jnp.int32(MODULUS)


def dft_left(matrix, x):
    digits = jnp.concatenate(split_digits(x), 0)
    sums = jnp.dot(matrix, digits, preferred_element_type=jnp.float32)
    rows = sums.shape[0] // 4
    return join_sums([sums[i * rows : (i + 1) * rows] for i in range(4)])


def dft_right(x, matrix):
    digits = jnp.concatenate(split_digits(x), 1)
    sums = jnp.dot(digits, matrix, preferred_element_type=jnp.float32)
    columns = sums.shape[1] // 4
    return join_sums([sums[:, i * columns : (i + 1) * columns] for i in range(4)])


def canonical(x):
    return jnp.where(x < 0, x + MODULUS, x)


def traced_left_matrix(base):
    lifted = [base] + [times_const(base, 1 << (8 * a)) for a in range(1, 4)]
    return jnp.concatenate(split_digits(jnp.concatenate(lifted, 1)), 0)


def shift_powers(shift):
    squares = [shift]
    for _ in range(LOG_TRACE - 1):
        squares.append(times(squares[-1], squares[-1], lift(squares[-1])))
    index = jnp.arange(256, dtype=jnp.int32)
    vectors = []
    for group in range(3):
        result = jnp.ones((256,), jnp.int32)
        for bit in range(min(8, LOG_TRACE - 8 * group)):
            square = squares[8 * group + bit]
            taken = times(result, square, lift(square))
            result = jnp.where((index >> bit) & 1 == 1, taken, result)
        vectors.append(result)
    return vectors[0], vectors[1], vectors[2][:128]


def first_kernel(x_ref, matrix_ref, plain_ref, lifted_ref, out_ref):
    y = dft_left(matrix_ref[...], x_ref[...])
    out_ref[...] = times(y, plain_ref[...], lifted_ref[...])


def last_kernel(x_ref, matrix_ref, plain_ref, lifted_ref, out_ref):
    x = times(x_ref[...], plain_ref[...], lifted_ref[...])
    out_ref[...] = canonical(dft_left(matrix_ref[...], x))


def line_pass(body, x, matrix, plain, lifted, width):
    rows, columns = x.shape
    block = pl.BlockSpec((rows, width), lambda i: (0, i))
    return pl.pallas_call(
        body,
        grid=(columns // width,),
        in_specs=[block, pl.BlockSpec(matrix.shape, lambda i: (0, 0)), block, block],
        out_specs=block,
        out_shape=jax.ShapeDtypeStruct(x.shape, jnp.int32),
        compiler_params=pltpu.CompilerParams(vmem_limit_bytes=VMEM_BYTES),
    )(x, matrix, plain, lifted)


def middle_kernel(group, x_ref, m2, p2, l2, m3, pw, lw, m4, p4, l4, m5, out_ref):
    lines = [x_ref[g] for g in range(group)]
    z = dft_left(m2[...], jnp.concatenate(lines, 1))
    lines = [times(z[:, g * 128 : (g + 1) * 128], p2[...], l2[...]) for g in range(group)]
    c = dft_right(jnp.concatenate(lines, 0), m3[...])
    lines = [times(c[g * 256 : (g + 1) * 256], pw[...], lw[...]) for g in range(group)]
    y = dft_right(jnp.concatenate(lines, 0), m4[...])
    lines = [times(y[g * 256 : (g + 1) * 256], p4[...], l4[...]) for g in range(group)]
    v = dft_left(m5[...], jnp.concatenate(lines, 1))
    for g in range(group):
        out_ref[g] = v[:, g * 256 : (g + 1) * 256]


def middle_pass(x, tables, group):
    count = x.shape[0]
    whole = [pl.BlockSpec(t.shape, lambda i: (0, 0)) for t in tables]
    return pl.pallas_call(
        functools.partial(middle_kernel, group),
        grid=(count // group,),
        in_specs=[pl.BlockSpec((group, 256, 128), lambda i: (i, 0, 0))] + whole,
        out_specs=pl.BlockSpec((group, 256, 256), lambda i: (i, 0, 0)),
        out_shape=jax.ShapeDtypeStruct((count, 256, 256), jnp.int32),
        compiler_params=pltpu.CompilerParams(vmem_limit_bytes=VMEM_BYTES),
    )(x, *tables)


def from_limbs(trace_limbs):
    low_part = (trace_limbs[0] * 65536.0).astype(jnp.int32)
    high_part = (trace_limbs[1] * 65536.0).astype(jnp.int32)
    joined = high_part * 65536 + low_part
    return jnp.where(joined >= MODULUS, joined - MODULUS, joined)


def to_limbs(field_values):
    return (
        jnp.stack(
            [(field_values & 65535).astype(jnp.float32), (field_values >> 16).astype(jnp.float32)]
        )
        / 65536.0
    )


def exchange(x):
    return lax.all_to_all(x, "rows", split_axis=0, concat_axis=0, tiled=True)


def on_device(trace_limbs, coset_shift):
    devices = lax.axis_size("rows")
    position = lax.axis_index("rows")
    per = 256 // devices
    chunk = 32768 // devices
    ext_len = 2 * TRACE_LEN
    back = inverse_of(unity_root(TRACE_LEN))
    back_256 = inverse_of(unity_root(256))
    ahead = unity_root(ext_len)

    p1, l1 = np_pair(outer_powers(back, 256, chunk, TRACE_LEN))
    p6, l6 = np_pair(outer_powers(ahead, 256, 2 * chunk, ext_len))
    step1 = np_powers(pow(back, chunk, MODULUS), 256 * devices)
    step6 = np_powers(pow(ahead, 2 * chunk, MODULUS), 256 * devices)
    exponents = np.arange(devices)[:, None] * np.arange(256)[None, :] % (256 * devices)
    row1 = np.stack(np_pair(step1[exponents]))
    row6 = np.stack(np_pair(step6[exponents]))
    dft_back = outer_powers(back_256, 256, 256, 256)
    dft_ahead = outer_powers(unity_root(256), 256, 256, 256)

    row1 = lax.dynamic_index_in_dim(jnp.asarray(row1), position, 1, False)
    m1 = traced_left_matrix(
        times(jnp.asarray(np_pair(dft_back)[0]), row1[0][:, None], row1[1][:, None])
    )
    s1, s2, s3 = shift_powers(coset_shift[0])
    s3 = times_const(s3, inverse_of(TRACE_LEN))
    pw = times(s2[:, None], s3[None, :], lift(s3)[None, :])
    lw = lift(pw)
    row6 = lax.dynamic_index_in_dim(jnp.asarray(row6), position, 1, False)
    row6 = times(s1, row6[0], row6[1])
    m6 = traced_left_matrix(
        times(jnp.asarray(np_pair(dft_ahead)[0]), row6[None, :], lift(row6)[None, :])
    )

    p2, l2 = np_pair(outer_powers(inverse_of(unity_root(32768)), 256, 128, 32768))
    p4, l4 = np_pair(outer_powers(unity_root(65536), 256, 256, 65536))
    m2 = np_left_matrix(dft_back)
    m3 = np_right_matrix(outer_powers(inverse_of(unity_root(128)), 128, 128, 128))
    m4 = np_right_matrix(dft_ahead[:128])
    m5 = np_left_matrix(dft_ahead)

    values = from_limbs(trace_limbs)
    x = values.reshape(per, devices, chunk).transpose(1, 0, 2)
    x = exchange(x).reshape(256, chunk)
    x = line_pass(first_kernel, x, m1, jnp.asarray(p1), jnp.asarray(l1), min(512, chunk))
    x = exchange(x.reshape(devices, per, chunk))
    x = x.reshape(devices, per, per, 128).transpose(1, 0, 2, 3).reshape(per, 256, 128)
    tables = [m2, p2, l2, m3, pw, lw, m4, p4, l4, m5]
    x = middle_pass(x, [jnp.asarray(t) for t in tables], 2)
    x = x.reshape(per, devices, per, 256).transpose(1, 0, 2, 3)
    x = exchange(x).reshape(256, 2 * chunk)
    x = line_pass(last_kernel, x, m6, jnp.asarray(p6), jnp.asarray(l6), min(512, 2 * chunk))
    x = exchange(x.reshape(devices, per, 2 * chunk))
    x = x.transpose(1, 0, 2).reshape(per * devices * 2 * chunk)
    return to_limbs(x)


def solution(mesh):
    placed = (P(None, ("cols", "rows")), P())
    return jax.shard_map(
        on_device, mesh=mesh, in_specs=placed, out_specs=P(None, ("cols", "rows")), check_vma=False
    )
```

time: 2830 us -> 895 us (0.32)
  other arithmetic: 1630 us -> 84.5 us
  local copies, waits for them, and re-layouts: 579 us -> 94.3 us
  Pallas kernels: 0 us -> 141 us
    select_n x93 -> x1, other arithmetic: 1250 us -> 0.08 us  [shift_powers(): result = jnp.where(index >> bit & 1 == 1, taken, result)]
    another operation x48 -> x0, local copies, waits for them, and re-layouts: 356 us -> none  [the longest x24 234 us: transform(): halves = leading.reshape(half_span, 2, groups * row_count)]
    pallas_call x0 -> x3, Pallas kernels: none -> 141 us  [the longest x1 87.2 us: middle_pass(): pl.pallas_call(functools.partial(middle_kernel, group), grid=(count // gr...]
    another operation x41 -> x0, other arithmetic: 138 us -> none  [the longest x24 117 us: transform(): jnp.stack([field_add(even_part, product), field_sub(even_part, product)], 0)]
    unnamed x198 -> x18, local copies, waits for them, and re-layouts: 114 us -> 17.5 us
    shift_right_arithmetic x25 -> x1, other arithmetic: 88.5 us -> 0.1 us  [times(): high = x >> 16]
    convert_element_type x99 -> x2, other arithmetic: 72.5 us -> 1.28 us  [split_digits(): digits.append((x - (above << 8)).astype(jnp.float32).astype(jnp.bfloat16))]
    all_to_all x5 -> x3, waiting for transfers between devices: 383 us -> 359 us  [exchange(): return lax.all_to_all(x, 'rows', split_axis=0, concat_axis=0, tiled=True)]
  transfers between devices with their start and end apart: 5 -> 3, of which waited for: 5 -> 3; matrix products, arithmetic and copies ran while one was open for 6% -> 1% of each run, Pallas kernels for 0% -> 0%
where the time goes in v1:
time: 895 us; the launch traced here: 886 us
  waiting for transfers between devices  359 us (40%)
  blocking collectives  188 us (21%)
  Pallas kernels  141 us (16%)
  local copies, waits for them, and re-layouts  94.3 us (11%)
  other arithmetic  84.5 us (9%)
  starting transfers between devices  17.7 us (2%)
    all_to_all x3, waiting for transfers between devices, exchange(): return lax.all_to_all(x, 'rows', split_axis=0, concat_axis=0, tiled=True)  359 us
    all_to_all x1, blocking collectives, exchange(): return lax.all_to_all(x, 'rows', split_axis=0, concat_axis=0, tiled=True)  188 us
    pallas_call x1, Pallas kernels, middle_pass(): pl.pallas_call(functools.partial(middle_kernel, group), grid=(count // gr...  87.2 us
    pallas_call x2, Pallas kernels, line_pass(): pl.pallas_call(body, grid=(columns // width,), in_specs=[block, pl.BlockS...  53.5 us
    add x1, other arithmetic, from_limbs(): joined = high_part * 65536 + low_part  39 us
    convert_element_type x2, local copies, waits for them, and re-layouts, to_limbs(): (field_values >> 16).astype(jnp.float32)  30.2 us
    convert_element_type x2, local copies, waits for them, and re-layouts, to_limbs(): (field_values & 65535).astype(jnp.float32)  30 us
    div x1, other arithmetic, to_limbs(): jnp.stack([(field_values & 65535).astype(jnp.float32), (field_values >> 1...  19.8 us
  transfers between devices with their start and end apart: 3, of which 3 were waited for; matrix products, arithmetic and copies ran while one was open for 1% of the time, Pallas kernels for 0%

profile of v1, /device:TPU:0, one launch (start us, length us, event | category | flops | bytes accessed | tf_op | source)
XLA Modules:
  0.0 885.9 jit_solution(7710668012870970951)
XLA Ops:
  0.0 39.0 %add_reduce_fusion = s32[1048576]{0:T(1024)} fusion(f32[2,1048576]{1,0:T(2,128)} %param.18), kind=kLoop, calls=%fused_computation.6 | loop fusion | flops 6291456 | bytes 12582912 | tf_op jit(solution)/shard_map/add | solution.py:203
  39.0 4.9 add.1453
  43.9 7.1 fusion
  51.1 7.4 all-to-all-start
  58.5 0.8 constant_dynamic-slice_fusion
  59.3 0.3 multiply_subtract_fusion.6
  59.6 0.2 multiply_subtract_fusion.5
  59.9 0.6 convert_convert_fusion.7
  60.5 1.5 pad_maximum_fusion.matrix_ref
  62.0 89.7 %all-to-all-done = s32[8,32,4096]{2,1,0:T(8,128)} async-done(((s32[8,32,4096]{2,1,0:T(8,128)}), s32[8,32,4096]{2,1,0:T(8,128)}, u32[]{:S(2)}, u32[]{:S(2)}) %all-to-all-start) | async-done | bytes 4194336 | tf_op jit(solution)/shard_map/all_to_all | solution.py:217
  151.8 18.7 %shard_map.172 = s32[256,4096]{1,0:T(8,128)} custom-call(s32[256,4096]{1,0:T(8,128)} %bitcast.1.x_ref, bf16[1024,1024]{1,0:T(8,128)(2,1)} %pad_maximum_fusion.matrix_ref, s32[256,4096]{1,0:T(8,128)} %constant.90.clone.plain_ref, s32[256,4096]{1,0:T(8,128)} %constant.91.clone.lifted_ref), custom_call_target="tpu_custom_call" | custom-call | tf_op jit(solution)/shard_map/pallas_call | solution.py:164
  170.4 4.8 all-to-all-start.1
  176.7 0.9 multiply_subtract_fusion.8
  177.6 90.2 %all-to-all-done.1 = s32[8,32,4096]{2,1,0:T(8,128)} async-done(((s32[8,32,4096]{2,1,0:T(8,128)}), s32[8,32,4096]{2,1,0:T(8,128)}, u32[]{:S(2)}, u32[]{:S(2)}) %all-to-all-start.1) | async-done | bytes 4194336 | tf_op jit(solution)/shard_map/all_to_all | solution.py:217
  267.8 2.9 copy.27
  270.7 2.6 copy.26
  273.3 87.2 %shard_map.173 = s32[32,256,256]{2,1,0:T(8,128)} custom-call(s32[32,256,128]{2,1,0:T(8,128)} %bitcast.37, bf16[1024,1024]{1,0:T(8,128)(2,1)} %constant.92.clone.m2, s32[256,128]{1,0:T(8,128)} %constant.29.clone.p2, s32[256,128]{1,0:T(8,128)} %constant.30.clone.l2, bf16[512,512]{1,0:T(8,128)(2,1)} %constant.31.clone.m3, s32[256,128]{1,0:T(8,128)} %get-tuple-element.36.pw, ...), custom_call_target="tpu_custom_call" | custom-call | tf_op jit(solution)/shard_map/pallas_call | solution.py:190
  360.5 8.3 copy.31
  368.8 5.5 all-to-all-start.2
  374.5 0.5 multiply_subtract_fusion.3
  375.0 0.6 convert_convert_fusion.3
  375.6 1.5 pad_maximum_fusion.1.matrix_ref
  377.1 179.2 %all-to-all-done.2 = s32[8,32,32,256]{3,2,1,0:T(8,128)} async-done(((s32[8,32,32,256]{3,2,1,0:T(8,128)}), s32[8,32,32,256]{3,2,1,0:T(8,128)}, u32[]{:S(2)}, u32[]{:S(2)}) %all-to-all-start.2) | async-done | bytes 8388640 | tf_op jit(solution)/shard_map/all_to_all | solution.py:217
  556.3 14.5 %copy.28 = s32[32,8,32,256]{3,1,2,0:T(8,128)} copy(s32[32,8,32,256]{3,2,1,0:T(8,128)} %bitcast.21) | data formatting | bytes 16777216
  570.9 34.9 %shard_map.174 = s32[256,8192]{1,0:T(8,128)} custom-call(s32[256,8192]{1,0:T(8,128)} %bitcast.33, bf16[1024,1024]{1,0:T(8,128)(2,1)} %pad_maximum_fusion.1.matrix_ref, s32[256,8192]{1,0:T(8,128)} %constant.36.clone.plain_ref, s32[256,8192]{1,0:T(8,128)} %constant.37.clone.lifted_ref), custom_call_target="tpu_custom_call" | custom-call | tf_op jit(solution)/shard_map/pallas_call | solution.py:164
  605.7 187.6 %all_to_all.20 = s32[8,32,8192]{2,1,0:T(8,128)} all-to-all(s32[8,32,8192]{2,1,0:T(8,128)} %bitcast.34), channel_id=1, replica_groups=mesh['rows'=8,'cols'=4] {'rows'}, dimensions={0} | all-to-all | bytes 16777216 | tf_op jit(solution)/shard_map/all_to_all | solution.py:217
  793.3 12.0 %convert_bitcast_fusion.1 = (f32[32,8,8192]{2,0,1:T(8,128)}, f32[32,8,8192]{2,0,1:T(8,128)}) fusion(s32[8,32,8192]{2,1,0:T(8,128)} %all_to_all.20), kind=kLoop, calls=%fused_computation.4 | loop fusion | flops 8388608 | bytes 25165824 | tf_op jit(solution)/shard_map/convert_element_type | solution.py:210
  805.3 11.5 %copy.24 = f32[32,8,8192]{2,1,0:T(8,128)} copy(f32[32,8,8192]{2,0,1:T(8,128)} %get-tuple-element.15) | data formatting | bytes 16777216 | tf_op jit(solution)/shard_map/convert_element_type | solution.py:210
  816.8 18.6 %convert_element_type.1925 = f32[1,2097152]{1,0:T(1,128)} reshape(f32[32,8,8192]{2,1,0:T(8,128)} %copy.24) | data formatting | bytes 16777216 | tf_op jit(solution)/shard_map/convert_element_type | solution.py:210
  835.4 11.6 %copy.25 = f32[32,8,8192]{2,1,0:T(8,128)} copy(f32[32,8,8192]{2,0,1:T(8,128)} %get-tuple-element.16) | data formatting | bytes 16777216 | tf_op jit(solution)/shard_map/convert_element_type | solution.py:210
  847.0 18.6 %convert_element_type.1928 = f32[1,2097152]{1,0:T(1,128)} reshape(f32[32,8,8192]{2,1,0:T(8,128)} %copy.25) | data formatting | bytes 16777216 | tf_op jit(solution)/shard_map/convert_element_type | solution.py:210
  865.6 19.8 %maximum_multiply_fusion = f32[2,2097152]{1,0:T(2,128)} fusion(f32[1,2097152]{1,0:T(1,128)} %convert_element_type.1928, f32[1,2097152]{1,0:T(1,128)} %convert_element_type.1925), kind=kLoop, calls=%fused_computation | loop fusion | flops 8388608 | bytes 33554432 | tf_op jit(solution)/shard_map/div | solution.py:209
  (25 shorter events, 0.4 us)
Async XLA Ops:
  51.1 8.2 copy-start
  51.1 8.2 copy-start.1
  51.1 8.2 copy-start.2
  51.1 8.2 copy-start.3
  51.1 100.7 %all-to-all-start = ((s32[8,32,4096]{2,1,0:T(8,128)}), s32[8,32,4096]{2,1,0:T(8,128)}, u32[]{:S(2)}, u32[]{:S(2)}) async-start(s32[8,32,4096]{2,1,0:T(8,128)} %fusion), calls=%async_computation | async-start | bytes 8388608 | tf_op jit(solution)/shard_map/all_to_all | solution.py:217
  170.4 97.3 %all-to-all-start.1 = ((s32[8,32,4096]{2,1,0:T(8,128)}), s32[8,32,4096]{2,1,0:T(8,128)}, u32[]{:S(2)}, u32[]{:S(2)}) async-start(s32[8,32,4096]{2,1,0:T(8,128)} %bitcast.39), calls=%async_computation.1 | async-start | bytes 8388608 | tf_op jit(solution)/shard_map/all_to_all | solution.py:217
  368.8 5.7 copy-start.4
  368.8 5.7 copy-start.5
  368.8 5.7 copy-start.6
  368.8 5.7 copy-start.7
  368.8 187.5 %all-to-all-start.2 = ((s32[8,32,32,256]{3,2,1,0:T(8,128)}), s32[8,32,32,256]{3,2,1,0:T(8,128)}, u32[]{:S(2)}, u32[]{:S(2)}) async-start(s32[8,32,32,256]{3,2,1,0:T(8,128)} %bitcast.36), calls=%async_computation.2 | async-start | bytes 16777216 | tf_op jit(solution)/shard_map/all_to_all | solution.py:217
